TPU v7x, 32 devices: a whole 2x2x4 slice. The times are simulated.
32 devices in a mesh: grp: 4 (over y, core), blk: 8 (over z, x).
Axes of the slice: x: 2, y: 2, z: 4, core: 2. Of those that a mesh axis runs over, the one named last changes fastest.
Arguments:
- embeddings: float32 [8192, 768], P(('grp', 'blk')), may hold values from -6 to 6
- owner: int32 [8192, 1], P(('grp', 'blk')), may hold values from 0 to 3; in each aligned block of 256 rows (0 to 255, 256 to 511, ...) at most 256 rows name the same one
- cluster: int32 [8192], P(('grp', 'blk')), may hold values from 0 to 1
- order: int32 [8192], P(('grp', 'blk')), may hold values from 0 to 8191, each once
Outputs:
- nearest: float32 [8192], P(('grp', 'blk'))
Inputs may be any that keep to these rules, and one draw needn't show every extreme that they name: `owner`: in the rows of one device no group is named by more than 256 rows, a bound that some block reaches.
All inputs are finite; a program needn't handle non-finite values.
Results may differ from a plain program's by a relative error of at most 0.0013.
Values may be sent and summed in bfloat16 or wider, within the bound.
A program may use at most 128 MiB of HBM per device.

v0:
```python
import jax
import jax.numpy as jnp
from jax import lax
from jax.sharding import PartitionSpec as P


def masked_best(queries, query_clus, query_order, keys, key_clus, key_order):
    scores = lax.dot_general(
        queries, keys, (((1,), (1,)), ((), ())), preferred_element_type=jnp.float32
    )
    forward = (query_clus[:, None] == key_clus[None, :]) & (key_clus[None, :] >= 0)
    earlier = forward & (key_order[None, :] < query_order[:, None])
    later = forward & (query_order[:, None] < key_order[None, :])
    low = jnp.float32(-1.0)
    rows_best = jnp.max(jnp.where(earlier, scores, low), axis=1)
    cols_best = jnp.max(jnp.where(later, scores, low), axis=0)
    return (rows_best, cols_best)


def local(embeddings, owner, cluster, order):
    groups = lax.axis_size("grp")
    row_count = embeddings.shape[0]
    width = embeddings.shape[1]
    capacity = max(2, 4 * row_count // groups)
    unit = (
        embeddings * lax.rsqrt(jnp.sum(embeddings * embeddings, axis=1, keepdims=True) + 1e-06)
    ).astype(jnp.bfloat16)
    target = owner[:, 0]
    onehot = (target[:, None] == jnp.arange(groups, dtype=jnp.int32)[None, :]).astype(jnp.int32)
    position = jnp.sum((jnp.cumsum(onehot, axis=0) - 1) * onehot, axis=1)
    flat = target * capacity + position
    slots = groups * capacity
    send_emb = (
        jnp.zeros((slots, width), jnp.bfloat16).at[flat].set(unit).reshape(groups, capacity, width)
    )
    send_clus = jnp.full((slots,), -1, jnp.int32).at[flat].set(cluster).reshape(groups, capacity)
    send_order = jnp.zeros((slots,), jnp.int32).at[flat].set(order).reshape(groups, capacity)
    got_emb, got_clus, got_order = (
        lax.all_to_all(send_emb, "grp", split_axis=0, concat_axis=0, tiled=True),
        lax.all_to_all(send_clus, "grp", split_axis=0, concat_axis=0, tiled=True),
        lax.all_to_all(send_order, "grp", split_axis=0, concat_axis=0, tiled=True),
    )
    keys = got_emb.reshape(slots, width)
    key_clus = got_clus.reshape(slots)
    key_order = got_order.reshape(slots)
    found, unused = masked_best(
        keys,
        key_clus,
        key_order,
        lax.all_gather(keys, "blk", axis=0, tiled=True),
        lax.all_gather(key_clus, "blk", axis=0, tiled=True),
        lax.all_gather(key_order, "blk", axis=0, tiled=True),
    )
    best = jnp.maximum(jnp.full((slots,), -1.0, jnp.float32), found)
    home = lax.all_to_all(
        best.reshape(groups, capacity), "grp", split_axis=0, concat_axis=0, tiled=True
    )
    return home.reshape(slots)[flat]


def solution(mesh):
    placed = (
        P(("grp", "blk"), None),
        P(("grp", "blk"), None),
        P(("grp", "blk")),
        P(("grp", "blk")),
    )
    return jax.shard_map(
        local, mesh=mesh, in_specs=placed, out_specs=P(("grp", "blk")), check_vma=False
    )
```

profile of v0, /device:TPU:0, one launch (start us, length us, event | category | flops | bytes accessed | tf_op | source)
XLA Modules:
  0.0 253.3 jit_solution(2120076414624383012)
XLA Ops:
  6.5 0.0 all-gather.2.cloned.1.call-start
  6.5 0.7 compare_convert_fusion
  7.2 1.2 reduce-window.6
  8.4 0.1 slice.10
  8.5 0.1 copy.9
  8.6 0.1 copy.10
  8.7 0.1 add_bitcast_fusion
  8.8 0.7 fusion.4
  9.5 0.7 compare_select_fusion
  10.2 1.3 multiply_reduce_fusion
  11.5 2.8 %scatter_custom_fusion.2 = bf16[1024,768]{1,0:T(8,128)(2,1)S(1)} fusion(s32[256]{0:T(256)S(1)} %bitcast.39, bf16[]{:T(256)} %constant.13.clone.1, f32[256,768]{1,0:T(8,128)} %param.4, f32[256]{0:T(256)S(1)} %add_rsqrt_fusion), kind=kCustom, calls=%fused_computation.7 | custom fusion | flops 393216 | bytes 2360322 | tf_op jit(solution)/shard_map/scatter | solution.py:34
  14.3 24.2 %all_to_all.29 = bf16[4,256,768]{2,1,0:T(8,128)(2,1)} all-to-all(bf16[4,256,768]{2,1,0:T(8,128)(2,1)S(1)} %bitcast.32), channel_id=1, replica_groups=mesh['grp'=4,'blk'=8] {'grp'}, dimensions={0} | all-to-all | bytes 3145728 | tf_op jit(solution)/shard_map/all_to_all | solution.py:39
  38.5 0.0 all-gather.2.cloned.1.call-update
  38.5 2.1 scatter_custom_fusion
  40.6 3.2 %all-to-all-start = ((s32[4,1,256]{2,1,0:T(1,128)}), s32[4,1,256]{2,1,0:T(1,128)S(1)}, u32[]{:S(2)}, u32[]{:S(2)}) async-start(s32[4,1,256]{2,1,0:T(1,128)} %bitcast.6), calls=%async_computation | async-start | bytes 8192 | tf_op jit(solution)/shard_map/all_to_all | solution.py:40
  43.9 2.1 scatter_custom_fusion.1
  46.0 1.5 all-to-all-done
  47.5 3.2 %all-to-all-start.1 = ((s32[4,1,256]{2,1,0:T(1,128)}), s32[4,1,256]{2,1,0:T(1,128)S(1)}, u32[]{:S(2)}, u32[]{:S(2)}) async-start(s32[4,1,256]{2,1,0:T(1,128)} %bitcast.8), calls=%async_computation.1 | async-start | bytes 8192 | tf_op jit(solution)/shard_map/all_to_all | solution.py:41
  50.7 31.9 %all_gather.9 = s32[8192]{0:T(1024)S(1)} all-gather(s32[1024]{0:T(1024)S(1)} %bitcast.33), channel_id=1, replica_groups=mesh['grp'=4,'blk'=8] {'blk'}, dimensions={0}, use_global_device_ids=true | all-gather | bytes 36864 | tf_op jit(solution)/shard_map/all_gather | solution.py:51
  82.6 0.0 all-to-all-done.1
  82.6 30.8 %all_gather.10 = s32[8192]{0:T(1024)S(1)} all-gather(s32[1024]{0:T(1024)S(1)} %bitcast.35), channel_id=1, replica_groups=mesh['grp'=4,'blk'=8] {'blk'}, dimensions={0}, use_global_device_ids=true | all-gather | bytes 36864 | tf_op jit(solution)/shard_map/all_gather | solution.py:52
  113.3 102.9 %all-gather.2.cloned.1.call-done = bf16[8192,768]{1,0:T(8,128)(2,1)} async-done(((bf16[1024,768]{1,0:T(8,128)(2,1)}), bf16[8192,768]{1,0:T(8,128)(2,1)}) %all-gather.2.cloned.1.call-update) | async-done | bytes 12582928 | tf_op jit(solution)/shard_map/all_gather | solution.py:50
  216.3 20.7 %select_reduce_fusion = f32[1024]{0:T(1024)S(1)} fusion(bf16[1024,768]{1,0:T(8,128)(2,1)} %bitcast.31, bf16[8192,768]{1,0:T(8,128)(2,1)} %all-gather.2.cloned.1.call-done, s32[8192]{0:T(1024)S(1)} %all_gather.10, s32[8192]{0:T(1024)S(1)} %all_gather.9, s32[1024]{0:T(1024)S(1)} %bitcast.36, s32[1024]{0:T(1024)S(1)} %bitcast.34, ...), kind=kOutput, calls=%fused_computation.4 | convolution fusion | flops 12935232512 | bytes 14241792 | tf_op jit(solution)/shard_map/dot_general | solution.py:8
  237.0 0.6 broadcast_maximum_fusion
  237.5 3.2 %all-to-all-start.3 = ((f32[4,1,256]{2,1,0:T(1,128)}), f32[4,1,256]{2,1,0:T(1,128)S(1)}, u32[]{:S(2)}, u32[]{:S(2)}) async-start(f32[4,1,256]{2,1,0:T(1,128)} %bitcast.12), calls=%async_computation.3 | async-start | bytes 8192 | tf_op jit(solution)/shard_map/all_to_all | solution.py:55
  240.8 3.7 %all-to-all-done.3 = f32[4,1,256]{2,1,0:T(1,128)S(1)} async-done(((f32[4,1,256]{2,1,0:T(1,128)}), f32[4,1,256]{2,1,0:T(1,128)S(1)}, u32[]{:S(2)}, u32[]{:S(2)}) %all-to-all-start.3) | async-done | bytes 4128 | tf_op jit(solution)/shard_map/all_to_all | solution.py:55
  244.6 1.9 gather_fusion
  (5 shorter events, 0.1 us)
Async XLA Ops:
  6.5 209.7 %all-gather.2.cloned.1.call-start = ((), (), s32[]{:S(2)}) async-start(), calls=%async_computation.4 | async-start | bytes 14155776 | tf_op jit(solution)/shard_map/all_gather | solution.py:50
  40.6 6.8 %all-to-all-start = ((s32[4,1,256]{2,1,0:T(1,128)}), s32[4,1,256]{2,1,0:T(1,128)S(1)}, u32[]{:S(2)}, u32[]{:S(2)}) async-start(s32[4,1,256]{2,1,0:T(1,128)} %bitcast.6), calls=%async_computation | async-start | bytes 8192 | tf_op jit(solution)/shard_map/all_to_all | solution.py:40
  47.5 35.1 %all-to-all-start.1 = ((s32[4,1,256]{2,1,0:T(1,128)}), s32[4,1,256]{2,1,0:T(1,128)S(1)}, u32[]{:S(2)}, u32[]{:S(2)}) async-start(s32[4,1,256]{2,1,0:T(1,128)} %bitcast.8), calls=%async_computation.1 | async-start | bytes 8192 | tf_op jit(solution)/shard_map/all_to_all | solution.py:41
  237.5 7.0 %all-to-all-start.3 = ((f32[4,1,256]{2,1,0:T(1,128)}), f32[4,1,256]{2,1,0:T(1,128)S(1)}, u32[]{:S(2)}, u32[]{:S(2)}) async-start(f32[4,1,256]{2,1,0:T(1,128)} %bitcast.12), calls=%async_computation.3 | async-start | bytes 8192 | tf_op jit(solution)/shard_map/all_to_all | solution.py:55
Sparse Core Ops, SparseCore 0:
  38.6 177.5 all-gather.1
where the time goes:
time: 254 us; the launch traced here: 253 us
  waiting for transfers between devices  108 us (43%)
  blocking collectives  86.8 us (34%)
  matrix products  20.7 us (8%)
  between operations  13.5 us (5%)
  starting transfers between devices  9.71 us (4%)
  other arithmetic  8.03 us (3%)
  local copies, waits for them, and re-layouts  6.46 us (3%)
    all_gather x1, waiting for transfers between devices, local(): lax.all_gather(keys, 'blk', axis=0, tiled=True)  103 us
    all_gather x1, blocking collectives, local(): lax.all_gather(key_clus, 'blk', axis=0, tiled=True)  31.9 us
    all_gather x1, blocking collectives, local(): lax.all_gather(key_order, 'blk', axis=0, tiled=True)  30.8 us
    all_to_all x1, blocking collectives, local(): lax.all_to_all(send_emb, 'grp', split_axis=0, concat_axis=0, tiled=True)  24.2 us
    dot_general x1, matrix products, masked_best(): lax.dot_general(queries, keys, (((1,), (1,)), ((), ())), preferred_elemen...  20.7 us
  transfers between devices with their start and end apart: 4, of which 3 were waited for; matrix products, arithmetic and copies ran while one was open for 2% of the time, Pallas kernels for 0%

commit v1 on v0

v1 whole, which is shorter than its diff:
```python
import functools

import jax
import jax.numpy as jnp
from jax import lax
from jax.experimental import pallas as pl
from jax.experimental.pallas import tpu as pltpu
from jax.sharding import PartitionSpec as P

MESH = pl.DeviceIdType.MESH
CHUNKS = 4


def sizes(groups, blocks):
    planes = blocks // 2
    return groups // 2, planes, groups * 2, planes // 2


def kernel(groups, blocks, emb, own_r, clu_r, ord_r, out,
           rows, line, meta_p, meta_z, row_lo, row_key, row_acc, col_acc,
           row_in, col_in, row_out,
           send, meta_recv_p, meta_recv_z, plane_recv, up_recv, down_recv,
           row_send, col_send, row_recv, col_recv):
    n = emb.shape[0]
    half, part = n // 2, n // CHUNKS
    ys, zs, ps, mid = sizes(groups, blocks)
    ups, downs = mid, zs - mid - 1
    total = n * groups * blocks
    g, b = lax.axis_index("grp"), lax.axis_index("blk")
    y, c, z, x = g // 2, g % 2, b // 2, b % 2
    x_other, c_other = 1 - x, 1 - c

    def place(x, y, c):
        return (x * ys + y) * 2 + c

    def device(x, y, c, z):
        return (y * 2 + c, z * 2 + x)

    def plane_device(p):
        return device(p // (2 * ys), (p // 2) % ys, p % 2, z)

    def y_peer(d):
        return lax.rem(y + d, ys)

    me = place(x, y, c)
    used = [0]
    started = []

    def copy(src, dst, recv, to, cond=None):
        index = used[0]
        used[0] += 1
        made = pltpu.make_async_remote_copy(
            src_ref=src, dst_ref=dst, send_sem=send.at[index], recv_sem=recv,
            device_id=to, device_id_type=MESH)
        started.append((made, cond))
        if cond is None:
            made.start()
        else:
            pl.when(cond)(made.start)

    def arrived(dst, recv):
        pltpu.make_async_remote_copy(
            src_ref=dst, dst_ref=dst, send_sem=send.at[0], recv_sem=recv,
            device_id=device(x_other, y, c, z), device_id_type=MESH).wait_recv()

    barrier = pltpu.get_barrier_semaphore()
    for d in range(1, ps):
        pl.semaphore_signal(barrier, inc=1, device_id=plane_device(lax.rem(me + d, ps)),
                            device_id_type=MESH)
    for d in range(1, zs):
        pl.semaphore_signal(barrier, inc=1, device_id=device(x, y, c, lax.rem(z + d, zs)),
                            device_id_type=MESH)

    e = emb[...]
    rows[me] = (e * lax.rsqrt(jnp.sum(e * e, axis=1, keepdims=True) + 1e-6)).astype(jnp.bfloat16)
    low = ((own_r[...] * 2 + clu_r[...]) * total).astype(jnp.float32)
    key = low + ord_r[...].astype(jnp.float32)
    first = lax.broadcasted_iota(jnp.int32, (8, n), 0) == 0
    meta = jnp.where(first, jnp.broadcast_to(low, (8, n)), jnp.broadcast_to(key, (8, n)))
    meta_p[me] = meta
    meta_z[z] = meta
    pl.semaphore_wait(barrier, ps - 1 + zs - 1)

    def piece(p, h):
        return rows.at[p, pl.ds(h * half, half)]

    def send_piece(p, h, to):
        copy(piece(p, h), piece(p, h), plane_recv.at[p, h], to)

    def wait_piece(p, h):
        arrived(piece(p, h), plane_recv.at[p, h])

    to_x, to_c = device(x_other, y, c, z), device(x, y, c_other, z)

    def slot(s, q):
        return line.at[s, pl.ds(q * part, part)]

    def own(q):
        return rows.at[me, pl.ds(q * part, part)]

    above, below = device(x, y, c, lax.rem(z + 1, zs)), device(x, y, c, lax.rem(z + zs - 1, zs))

    for d in range(1, ps):
        p = lax.rem(me + d, ps)
        copy(meta_p.at[me], meta_p.at[me], meta_recv_p.at[me], plane_device(p))
    for d in range(1, zs):
        to = device(x, y, c, lax.rem(z + d, zs))
        copy(meta_z.at[z], meta_z.at[z], meta_recv_z.at[z], to)
    for q in range(CHUNKS):
        copy(own(q), slot(0, q), up_recv.at[0, q], above, z < mid)
        if downs:
            copy(own(q), slot(ups, q), down_recv.at[0, q], below, z > mid)
    for hx, hy in ((0, 1), (1, 0)):
        send_piece(me, hx, to_x)
        for d in range(1, ys):
            send_piece(me, hy, device(x, y_peer(d), c, z))
    for h in (0, 1):
        send_piece(me, h, to_c)

    row_acc[...] = jnp.full(row_acc.shape, -1.0, jnp.float32)
    col_acc[...] = jnp.full(col_acc.shape, -1.0, jnp.float32)
    for d in range(1, ps):
        p = lax.rem(me + d, ps)
        arrived(meta_p.at[p], meta_recv_p.at[p])
    for d in range(1, zs):
        o = lax.rem(z + d, zs)
        arrived(meta_z.at[o], meta_recv_z.at[o])

    def columns(p, carry):
        m = meta_p[p]
        row_lo[p] = jnp.broadcast_to(m[0:1], (128, n)).T
        row_key[p] = jnp.broadcast_to(m[1:2], (128, n)).T
        return carry

    lax.fori_loop(0, ps, columns, 0)

    def has_up(t):
        return z > t

    def has_down(t):
        return (z >= mid) & (zs - 1 - z > t)

    def step_line(t, q):
        if t < ups:
            @pl.when(has_up(t))
            def _():
                arrived(slot(t, q), up_recv.at[t, q])
            if t + 1 < ups:
                copy(slot(t, q), slot(t + 1, q), up_recv.at[t + 1, q], above, has_up(t) & (z < mid))
            copy(slot(t, q), slot(t, q), up_recv.at[t, q], above,
                 has_up(t) & (z >= mid) & (z < zs - 1))
        if t < downs:
            @pl.when(has_down(t))
            def _():
                arrived(slot(ups + t, q), down_recv.at[t, q])
            if t + 1 < downs:
                copy(slot(ups + t, q), slot(ups + t + 1, q), down_recv.at[t + 1, q], below,
                     has_down(t) & (z > mid))

    def fold(s):
        return jnp.max(s.reshape(n // 8, 8, s.shape[1]), axis=0)

    def scores(p, block):
        return lax.dot_general(rows[p], block[...], (((1,), (1,)), ((), ())),
                               preferred_element_type=jnp.float32)

    def within_plane():
        m = meta_z[z]

        def body(p, best):
            s = scores(p, rows.at[me])
            lo, k = row_lo[p], row_key[p]
            parts = []
            for w in range(0, n, 128):
                ok = (lo == m[0:1, w:w + 128]) & (k < m[1:2, w:w + 128])
                parts.append(fold(jnp.where(ok, s[:, w:w + 128], -1.0)))
            return jnp.maximum(best, jnp.concatenate(parts, axis=1))

        col_acc[z] = lax.fori_loop(0, ps, body, jnp.full((8, n), -1.0, jnp.float32))

    def between_planes(s_index, origin):
        m = meta_z[origin]

        def body(p, best):
            s = scores(p, line.at[s_index])
            lo, k = row_lo[p], row_key[p]
            acc = row_acc[p]
            parts = []
            for w in range(0, n, 128):
                same = jnp.where(lo == m[0:1, w:w + 128], s[:, w:w + 128], -1.0)
                later = k > m[1:2, w:w + 128]
                acc = jnp.maximum(acc, jnp.where(later, same, -1.0))
                parts.append(fold(jnp.where(later, -1.0, same)))
            row_acc[p] = acc
            return jnp.maximum(best, jnp.concatenate(parts, axis=1))

        col_acc[origin] = lax.fori_loop(0, ps, body, jnp.full((8, n), -1.0, jnp.float32))

    def compute_up(t):
        @pl.when(has_up(t))
        def _():
            between_planes(t, jnp.minimum(z, mid) - 1 - t)

    def compute_down(t):
        @pl.when(has_down(t))
        def _():
            between_planes(ups + t, z + 1 + t)

    def early_plane():
        wait_piece(place(x_other, y, c), 0)
        for d in range(1, ys):
            send_piece(place(x_other, y, c), 0, device(x, y_peer(d), c, z))
        for d in range(1, ys):
            p = place(x, y_peer(d), c)
            wait_piece(p, 1)
            send_piece(p, 1, to_x)
        send_piece(place(x_other, y, c), 0, to_c)
        for d in range(1, ys):
            send_piece(place(x, y_peer(d), c), 1, to_c)

    def late_plane():
        wait_piece(place(x_other, y, c), 1)
        send_piece(place(x_other, y, c), 1, to_c)
        for d in range(1, ys):
            p = place(x, y_peer(d), c)
            wait_piece(p, 0)
            send_piece(p, 0, to_c)

    def rest_of_plane():
        for d in range(1, ys):
            p = place(x_other, y_peer(d), c)
            for h in (0, 1):
                wait_piece(p, h)
                send_piece(p, h, to_c)
        for ox in (x, x_other):
            for d in range(ys):
                for h in (0, 1):
                    wait_piece(place(ox, y_peer(d), c_other), h)

    steps = max(ups, downs)
    for t in range(steps):
        for q in range(CHUNKS):
            step_line(t, q)
            if t == 0 and q == 1:
                early_plane()
            if t == 0 and q == CHUNKS - 1:
                late_plane()
            if t == 1 and q == 1:
                rest_of_plane()
                within_plane()
            if t == 1 and q == 2:
                compute_up(0)
        if t >= 2:
            compute_up(t - 1)
            if t - 2 < downs:
                compute_down(t - 2)
    for t in range(max(0, steps - 2), downs):
        compute_down(t)
    compute_up(ups - 1)

    def go_home(p, wait):
        made = pltpu.make_async_remote_copy(
            src_ref=row_out.at[p], dst_ref=row_in.at[me], send_sem=row_send.at[p],
            recv_sem=row_recv.at[me], device_id=plane_device(p), device_id_type=MESH)
        if wait:
            made.wait_send()
        else:
            made.start()

    def line_home(o):
        return pltpu.make_async_remote_copy(
            src_ref=col_acc.at[o], dst_ref=col_in.at[z], send_sem=col_send.at[o],
            recv_sem=col_recv.at[z], device_id=device(x, y, c, o), device_id_type=MESH)

    for d in range(1, zs):
        line_home(lax.rem(z + d, zs)).start()
    for d in range(1, ps + 1):
        p = lax.rem(me + d, ps)
        t = row_acc[p].T
        row_out[p] = jnp.max(t.reshape(16, 8, n), axis=0)
        if d < ps:
            go_home(p, False)
    best = jnp.maximum(row_out[me], col_acc[z])
    for d in range(1, zs):
        o = lax.rem(z + d, zs)
        arrived(col_in.at[o], col_recv.at[o])
        best = jnp.maximum(best, col_in[o])
    for d in range(1, ps):
        p = lax.rem(me + d, ps)
        arrived(row_in.at[p], row_recv.at[p])
        best = jnp.maximum(best, row_in[p])
    out[...] = jnp.max(best, axis=0, keepdims=True)

    for made, cond in started:
        if cond is None:
            made.wait_send()
        else:
            pl.when(cond)(made.wait_send)
    for d in range(1, zs):
        line_home(lax.rem(z + d, zs)).wait_send()
    for d in range(1, ps):
        go_home(lax.rem(me + d, ps), True)


def local(embeddings, owner, cluster, order):
    groups, blocks = lax.axis_size("grp"), lax.axis_size("blk")
    n, width = embeddings.shape
    ys, zs, ps, mid = sizes(groups, blocks)
    slots = mid + max(1, zs - mid - 1)
    f32, bf16 = jnp.float32, jnp.bfloat16
    sends = (ps + zs + CHUNKS * 2 + 4 + 2 * ys + 2 + ys + 3 * ys + 2 * ys
             + 3 * CHUNKS * slots)
    dma = pltpu.SemaphoreType.DMA
    found = pl.pallas_call(
        functools.partial(kernel, groups, blocks),
        out_shape=jax.ShapeDtypeStruct((1, n), f32),
        in_specs=[pl.BlockSpec(memory_space=pltpu.VMEM)] * 4,
        out_specs=pl.BlockSpec(memory_space=pltpu.VMEM),
        scratch_shapes=[
            pltpu.VMEM((ps, n, width), bf16),
            pltpu.VMEM((slots, n, width), bf16),
            pltpu.VMEM((ps, 8, n), f32),
            pltpu.VMEM((zs, 8, n), f32),
            pltpu.VMEM((ps, n, 128), f32),
            pltpu.VMEM((ps, n, 128), f32),
            pltpu.VMEM((ps, n, 128), f32),
            pltpu.VMEM((zs, 8, n), f32),
            pltpu.VMEM((ps, 8, n), f32),
            pltpu.VMEM((zs, 8, n), f32),
            pltpu.VMEM((ps, 8, n), f32),
            dma((sends,)),
            dma((ps,)),
            dma((zs,)),
            dma((ps, 2)),
            dma((mid, CHUNKS)),
            dma((max(1, zs - mid - 1), CHUNKS)),
            dma((ps,)),
            dma((zs,)),
            dma((ps,)),
            dma((zs,)),
        ],
        compiler_params=pltpu.CompilerParams(
            collective_id=0, has_side_effects=True, vmem_limit_bytes=40 * 1024 * 1024),
    )(embeddings, owner.reshape(1, n), cluster.reshape(1, n), order.reshape(1, n))
    return found.reshape(n)


def solution(mesh):
    placed = (
        P(("grp", "blk"), None),
        P(("grp", "blk"), None),
        P(("grp", "blk")),
        P(("grp", "blk")),
    )
    return jax.shard_map(
        local, mesh=mesh, in_specs=placed, out_specs=P(("grp", "blk")), check_vma=False
    )
```

time: 254 us -> 40.5 us (0.16)
  waiting for transfers between devices: 108 us -> 0 us
  blocking collectives: 86.8 us -> 0 us
  Pallas kernels: 0 us -> 37.9 us
  matrix products: 20.7 us -> 0 us
  between operations: 13.5 us -> 0.01 us
  starting transfers between devices: 9.71 us -> 0 us
  other arithmetic: 8.03 us -> 0 us
  local copies, waits for them, and re-layouts: 6.46 us -> 2.41 us
    all_gather x1 -> x0, waiting for transfers between devices: 103 us -> none  [local(): lax.all_gather(keys, 'blk', axis=0, tiled=True)]
    all_gather x2 -> x0, blocking collectives: 62.6 us -> none  [the longest x1 31.9 us: local(): lax.all_gather(key_clus, 'blk', axis=0, tiled=True)]
    pallas_call x0 -> x1, Pallas kernels: none -> 37.9 us  [local(): pl.pallas_call(functools.partial(kernel, groups, blocks), out_shape=jax.S...]
    all_to_all x1 -> x0, blocking collectives: 24.2 us -> none  [local(): lax.all_to_all(send_emb, 'grp', split_axis=0, concat_axis=0, tiled=True)]
    dot_general x1 -> x0, matrix products: 20.7 us -> none  [masked_best(): lax.dot_general(queries, keys, (((1,), (1,)), ((), ())), preferred_elemen...]
    all_to_all x3 -> x0, starting transfers between devices: 9.71 us -> none  [the longest x1 3.24 us: local(): lax.all_to_all(best.reshape(groups, capacity), 'grp', split_axis=0, conca...]
    all_to_all x3 -> x0, waiting for transfers between devices: 5.21 us -> none  [the longest x1 3.74 us: local(): lax.all_to_all(best.reshape(groups, capacity), 'grp', split_axis=0, conca...]
    scatter x2 -> x0, local copies, waits for them, and re-layouts: 4.25 us -> none  [the longest x1 2.13 us: local(): jnp.zeros((slots,), jnp.int32).at[flat].set(order).reshape(groups, capacity)]
  transfers between devices with their start and end apart: 4 -> 0, of which waited for: 3 -> 0; matrix products, arithmetic and copies ran while one was open for 2% -> 0% of each run, Pallas kernels for 0% -> 0%
where the time goes in v1:
time: 40.5 us; the launch traced here: 40.4 us
  Pallas kernels  37.9 us (94%)
  local copies, waits for them, and re-layouts  2.41 us (6%)
    pallas_call x1, Pallas kernels, local(): pl.pallas_call(functools.partial(kernel, groups, blocks), out_shape=jax.S...  37.9 us
    unnamed x9, local copies, waits for them, and re-layouts  2.41 us

profile of v1, /device:TPU:0, one launch (start us, length us, event | category | flops | bytes accessed | tf_op | source)
XLA Modules:
  0.0 40.4 jit_solution(12311964937075785542)
XLA Ops:
  0.0 0.0 copy-start.2
  0.0 0.0 copy-start.3
  0.0 0.0 copy-start.1
  0.0 0.7 %copy-done.2 = s32[256]{0:T(256)S(1)} copy-done((s32[256]{0:T(256)S(1)}, s32[256]{0:T(256)}, u32[]{:S(2)}) %copy-start.2) | copy-done | bytes 1048
  0.7 0.0 copy-done.3
  0.7 0.0 copy-done.1
  0.7 0.0 copy-start
  0.7 1.1 %copy-done = f32[256,768]{1,0:T(8,128)S(1)} copy-done((f32[256,768]{1,0:T(8,128)S(1)}, f32[256,768]{1,0:T(8,128)}, u32[]{:S(2)}) %copy-start) | copy-done | bytes 786456
  1.8 37.9 %shard_map.46 = f32[1,256]{1,0:T(1,128)S(1)} custom-call(f32[256,768]{1,0:T(8,128)S(1)} %copy-done, s32[1,256]{1,0:T(1,128)S(1)} %bitcast.5, s32[1,256]{1,0:T(1,128)S(1)} %bitcast.6, s32[1,256]{1,0:T(1,128)S(1)} %bitcast.7), custom_call_target="tpu_custom_call" | custom-call | tf_op jit(solution)/shard_map/pallas_call | solution.py:314
  39.8 0.6 %copy.6 = f32[256]{0:T(256)} copy(f32[256]{0:T(256)S(1)} %bitcast.4) | data formatting | bytes 2048
Async XLA Ops:
  0.0 0.7 %copy-start.2 = (s32[256]{0:T(256)S(1)}, s32[256]{0:T(256)}, u32[]{:S(2)}) copy-start(s32[256]{0:T(256)} %param.6) | copy-start | bytes 3076
  0.0 0.7 %copy-start.3 = (s32[256]{0:T(256)S(1)}, s32[256]{0:T(256)}, u32[]{:S(2)}) copy-start(s32[256]{0:T(256)} %param.7) | copy-start | bytes 3076
  0.0 0.7 %copy-start.1 = (s32[256,1]{0,1:T(1,128)S(1)}, s32[256,1]{0,1:T(1,128)}, u32[]{:S(2)}) copy-start(s32[256,1]{0,1:T(1,128)} %param.5) | copy-start | bytes 3076
  0.7 1.1 %copy-start = (f32[256,768]{1,0:T(8,128)S(1)}, f32[256,768]{1,0:T(8,128)}, u32[]{:S(2)}) copy-start(f32[256,768]{1,0:T(8,128)} %emb.1) | copy-start | bytes 2359300

commit v2 on v1

v2 whole, which is shorter than its diff:
```python
import functools

import jax
import jax.numpy as jnp
from jax import lax
from jax.experimental import pallas as pl
from jax.experimental.pallas import tpu as pltpu
from jax.sharding import PartitionSpec as P

MESH = pl.DeviceIdType.MESH
CHUNKS = 4


def sizes(groups, blocks):
    planes = blocks // 2
    return groups // 2, planes, groups * 2, planes // 2


def kernel(groups, blocks, emb_h, own_h, clu_h, ord_h, out,
           emb, info, rows, line, meta_p, meta_z, col_lo, col_key, col_wide,
           row_acc, col_out, row_in, col_in,
           load, send, meta_recv_p, meta_recv_z, plane_recv, up_recv, down_recv,
           row_send, col_send, row_recv, col_recv):
    n = emb.shape[0]
    half, part = n // 2, n // CHUNKS
    ys, zs, ps, mid = sizes(groups, blocks)
    ups, downs = mid, zs - mid - 1
    total = n * groups * blocks
    g, b = lax.axis_index("grp"), lax.axis_index("blk")
    y, c, z, x = g // 2, g % 2, b // 2, b % 2
    x_other, c_other = 1 - x, 1 - c

    def place(x, y, c):
        return (x * ys + y) * 2 + c

    def device(x, y, c, z):
        return (y * 2 + c, z * 2 + x)

    def plane_device(p):
        return device(p // (2 * ys), (p // 2) % ys, p % 2, z)

    def y_peer(d):
        return lax.rem(y + d, ys)

    me = place(x, y, c)
    used = [0]
    started = []

    def copy(src, dst, recv, to, cond=None):
        index = used[0]
        used[0] += 1
        made = pltpu.make_async_remote_copy(
            src_ref=src, dst_ref=dst, send_sem=send.at[index], recv_sem=recv,
            device_id=to, device_id_type=MESH)
        started.append((made, cond))
        if cond is None:
            made.start()
        else:
            pl.when(cond)(made.start)

    def arrived(dst, recv):
        pltpu.make_async_remote_copy(
            src_ref=dst, dst_ref=dst, send_sem=send.at[0], recv_sem=recv,
            device_id=device(x_other, y, c, z), device_id_type=MESH).wait_recv()

    loads = [pltpu.make_async_copy(src, info.at[i], load.at[i])
             for i, src in enumerate((own_h, clu_h, ord_h))]
    loads += [pltpu.make_async_copy(emb_h.at[pl.ds(q * part, part)],
                                    emb.at[pl.ds(q * part, part)], load.at[3 + q])
              for q in range(CHUNKS)]
    for made in loads:
        made.start()

    barrier = pltpu.get_barrier_semaphore()
    for d in range(1, ps):
        pl.semaphore_signal(barrier, inc=1, device_id=plane_device(lax.rem(me + d, ps)),
                            device_id_type=MESH)
    for d in range(1, zs):
        pl.semaphore_signal(barrier, inc=1, device_id=device(x, y, c, lax.rem(z + d, zs)),
                            device_id_type=MESH)

    for made in loads[:3]:
        made.wait()
    low = ((info[0] * 2 + info[1]) * total).astype(jnp.float32)
    key = low + info[2].astype(jnp.float32)
    first = lax.broadcasted_iota(jnp.int32, (8, n), 0) == 0
    meta = jnp.where(first, jnp.broadcast_to(low, (8, n)), jnp.broadcast_to(key, (8, n)))
    meta_p[me] = meta
    meta_z[z] = meta
    for q in range(CHUNKS):
        loads[3 + q].wait()
        e = emb[q * part:(q + 1) * part]
        rows[me, q * part:(q + 1) * part] = (
            e * lax.rsqrt(jnp.sum(e * e, axis=1, keepdims=True) + 1e-6)).astype(jnp.bfloat16)
    pl.semaphore_wait(barrier, ps - 1 + zs - 1)

    def piece(p, h):
        return rows.at[p, pl.ds(h * half, half)]

    def send_piece(p, h, to):
        copy(piece(p, h), piece(p, h), plane_recv.at[p, h], to)

    def wait_piece(p, h):
        arrived(piece(p, h), plane_recv.at[p, h])

    to_x, to_c = device(x_other, y, c, z), device(x, y, c_other, z)

    def slot(s, q):
        return line.at[s, pl.ds(q * part, part)]

    def own(q):
        return rows.at[me, pl.ds(q * part, part)]

    above, below = device(x, y, c, lax.rem(z + 1, zs)), device(x, y, c, lax.rem(z + zs - 1, zs))

    for q in range(CHUNKS):
        copy(own(q), slot(0, q), up_recv.at[0, q], above, z < mid)
        if downs:
            copy(own(q), slot(ups, q), down_recv.at[0, q], below, z > mid)
    for hx, hy in ((0, 1), (1, 0)):
        send_piece(me, hx, to_x)
        for d in range(1, ys):
            send_piece(me, hy, device(x, y_peer(d), c, z))
    for d in range(1, ps):
        p = lax.rem(me + d, ps)
        copy(meta_p.at[me], meta_p.at[me], meta_recv_p.at[me], plane_device(p))
    for d in range(1, zs):
        to = device(x, y, c, lax.rem(z + d, zs))
        copy(meta_z.at[z], meta_z.at[z], meta_recv_z.at[z], to)
    for h in (0, 1):
        send_piece(me, h, to_c)

    def has_up(t):
        return z > t

    def has_down(t):
        return (z >= mid) & (zs - 1 - z > t)

    def step_line(t, q):
        if t < ups:
            @pl.when(has_up(t))
            def _():
                arrived(slot(t, q), up_recv.at[t, q])
            if t + 1 < ups:
                copy(slot(t, q), slot(t + 1, q), up_recv.at[t + 1, q], above, has_up(t) & (z < mid))
            copy(slot(t, q), slot(t, q), up_recv.at[t, q], above,
                 has_up(t) & (z >= mid) & (z < zs - 1))
        if t < downs:
            @pl.when(has_down(t))
            def _():
                arrived(slot(ups + t, q), down_recv.at[t, q])
            if t + 1 < downs:
                copy(slot(ups + t, q), slot(ups + t + 1, q), down_recv.at[t + 1, q], below,
                     has_down(t) & (z > mid))

    def nth(j):
        k = j // 2
        return place(lax.rem(x + k // ys, 2), lax.rem(y + k, ys), lax.rem(c + j, 2))

    near, every = (0, 2 * (ys + 1)), (0, ps)
    far = (near[1], ps)

    def fold(s):
        return jnp.max(s.reshape(s.shape[0] // 8, 8, s.shape[1]), axis=0)

    def compute(block, origin, start, count, members, both):
        span = pl.ds(start, count)

        def body(j, carry):
            p = nth(j)
            s = lax.dot_general(block[span], rows[p], (((1,), (1,)), ((), ())),
                                preferred_element_type=jnp.float32)
            lo, k, m = col_lo[origin, span], col_key[origin, span], meta_p[p]
            best = col_wide[origin, span]
            parts = []
            for w in range(0, n, 128):
                same = jnp.where(lo == m[0:1, w:w + 128], s[:, w:w + 128], -1.0)
                later = m[1:2, w:w + 128] > k
                if both:
                    best = jnp.maximum(best, jnp.where(later, -1.0, same))
                    parts.append(fold(jnp.where(later, same, -1.0)))
                else:
                    best = jnp.maximum(best, jnp.where(m[1:2, w:w + 128] < k, same, -1.0))
            col_wide[origin, span] = best
            if both:
                row_acc[p] = jnp.maximum(row_acc[p], jnp.concatenate(parts, axis=1))
            return carry

        lax.fori_loop(members[0], members[1], body, 0, unroll=2)

    def compute_own(members):
        compute(rows.at[me], z, 0, n, members, False)

    def compute_up(t, members, start=0, count=n):
        @pl.when(has_up(t))
        def _():
            compute(line.at[t], jnp.minimum(z, mid) - 1 - t, start, count, members, True)

    def compute_down(t, members):
        if t < downs:
            @pl.when(has_down(t))
            def _():
                compute(line.at[ups + t], z + 1 + t, 0, n, members, True)

    def early_plane():
        wait_piece(place(x_other, y, c), 0)
        for d in range(1, ys):
            send_piece(place(x_other, y, c), 0, device(x, y_peer(d), c, z))
        for d in range(1, ys):
            p = place(x, y_peer(d), c)
            wait_piece(p, 1)
            send_piece(p, 1, to_x)
        send_piece(place(x_other, y, c), 0, to_c)
        for d in range(1, ys):
            send_piece(place(x, y_peer(d), c), 1, to_c)

    def late_plane():
        wait_piece(place(x_other, y, c), 1)
        send_piece(place(x_other, y, c), 1, to_c)
        for d in range(1, ys):
            p = place(x, y_peer(d), c)
            wait_piece(p, 0)
            send_piece(p, 0, to_c)
        for j in range(1, near[1], 2):
            for h in (0, 1):
                wait_piece(nth(j), h)

    def far_plane():
        for d in range(1, ys):
            p = place(x_other, y_peer(d), c)
            for h in (0, 1):
                wait_piece(p, h)
                send_piece(p, h, to_c)

    def far_sibling():
        for j in range(far[0] + 1, far[1], 2):
            for h in (0, 1):
                wait_piece(nth(j), h)

    row_acc[...] = jnp.full(row_acc.shape, -1.0, jnp.float32)
    col_wide[...] = jnp.full(col_wide.shape, -1.0, jnp.float32)
    for d in range(1, zs):
        o = lax.rem(z + d, zs)
        arrived(meta_z.at[o], meta_recv_z.at[o])
    for o in range(zs):
        m = meta_z[o]
        col_lo[o] = jnp.broadcast_to(m[0:1], (128, n)).T
        col_key[o] = jnp.broadcast_to(m[1:2], (128, n)).T
    for d in range(1, ps):
        p = lax.rem(me + d, ps)
        arrived(meta_p.at[p], meta_recv_p.at[p])

    last = ups - 1
    for t in range(ups):
        for q in range(CHUNKS):
            step_line(t, q)
            if (t, q) == (0, 1):
                early_plane()
            if (t, q) == (0, CHUNKS - 1):
                late_plane()
                compute_own(near)
            if (t, q) == (1, 0):
                compute_up(0, near)
            if (t, q) == (1, 1):
                far_plane()
                compute_down(0, near)
            if (t, q) == (1, 2):
                far_sibling()
                compute_own(far)
                compute_up(0, far)
                compute_down(0, far)
            if t > 1 and q == 1:
                compute_up(t - 1, every)
                compute_down(t - 1, every)
            if (t, q) == (last, 2):
                compute_up(last, every, 0, half)

    def line_home(o):
        return pltpu.make_async_remote_copy(
            src_ref=col_out.at[o], dst_ref=col_in.at[z], send_sem=col_send.at[o],
            recv_sem=col_recv.at[z], device_id=device(x, y, c, o), device_id_type=MESH)

    def finish_line(o, cond):
        @pl.when(cond)
        def _():
            col_out[o] = fold(col_wide[o].T)
            line_home(o).start()

    def plane_home(p):
        return pltpu.make_async_remote_copy(
            src_ref=row_acc.at[p], dst_ref=row_in.at[me], send_sem=row_send.at[p],
            recv_sem=row_recv.at[me], device_id=plane_device(p), device_id_type=MESH)

    for o in range(zs):
        finish_line(o, z != o if o else (z > 0) & (z < mid))
    compute_up(last, every, half, half)
    finish_line(0, z >= mid)
    for d in range(1, ps):
        plane_home(lax.rem(me + d, ps)).start()
    best = jnp.maximum(row_acc[me], fold(col_wide[z].T))
    for d in range(1, zs):
        o = lax.rem(z + d, zs)
        arrived(col_in.at[o], col_recv.at[o])
        best = jnp.maximum(best, col_in[o])
    for d in range(1, ps):
        p = lax.rem(me + d, ps)
        arrived(row_in.at[p], row_recv.at[p])
        best = jnp.maximum(best, row_in[p])
    out[...] = jnp.max(best, axis=0, keepdims=True)

    for made, cond in started:
        if cond is None:
            made.wait_send()
        else:
            pl.when(cond)(made.wait_send)
    for d in range(1, zs):
        line_home(lax.rem(z + d, zs)).wait_send()
    for d in range(1, ps):
        plane_home(lax.rem(me + d, ps)).wait_send()


def local(embeddings, owner, cluster, order):
    groups, blocks = lax.axis_size("grp"), lax.axis_size("blk")
    n, width = embeddings.shape
    ys, zs, ps, mid = sizes(groups, blocks)
    slots = mid + max(1, zs - mid - 1)
    f32, bf16 = jnp.float32, jnp.bfloat16
    sends = (ps + zs + CHUNKS * 2 + 4 + 2 * ys + 2 + ys + 3 * ys + 2 * ys
             + 3 * CHUNKS * slots)
    dma = pltpu.SemaphoreType.DMA
    found = pl.pallas_call(
        functools.partial(kernel, groups, blocks),
        out_shape=jax.ShapeDtypeStruct((1, n), f32),
        in_specs=[pl.BlockSpec(memory_space=pltpu.HBM)] * 4,
        out_specs=pl.BlockSpec(memory_space=pltpu.VMEM),
        scratch_shapes=[
            pltpu.VMEM((n, width), f32),
            pltpu.VMEM((3, 1, n), jnp.int32),
            pltpu.VMEM((ps, n, width), bf16),
            pltpu.VMEM((slots, n, width), bf16),
            pltpu.VMEM((ps, 8, n), f32),
            pltpu.VMEM((zs, 8, n), f32),
            pltpu.VMEM((zs, n, 128), f32),
            pltpu.VMEM((zs, n, 128), f32),
            pltpu.VMEM((zs, n, 128), f32),
            pltpu.VMEM((ps, 8, n), f32),
            pltpu.VMEM((zs, 8, n), f32),
            pltpu.VMEM((ps, 8, n), f32),
            pltpu.VMEM((zs, 8, n), f32),
            dma((3 + CHUNKS,)),
            dma((sends,)),
            dma((ps,)),
            dma((zs,)),
            dma((ps, 2)),
            dma((mid, CHUNKS)),
            dma((max(1, zs - mid - 1), CHUNKS)),
            dma((ps,)),
            dma((zs,)),
            dma((ps,)),
            dma((zs,)),
        ],
        compiler_params=pltpu.CompilerParams(
            collective_id=0, has_side_effects=True, vmem_limit_bytes=64 * 1024 * 1024 - 524288),
    )(embeddings, owner.reshape(1, n), cluster.reshape(1, n), order.reshape(1, n))
    return found.reshape(n)


def solution(mesh):
    placed = (
        P(("grp", "blk"), None),
        P(("grp", "blk"), None),
        P(("grp", "blk")),
        P(("grp", "blk")),
    )
    return jax.shard_map(
        local, mesh=mesh, in_specs=placed, out_specs=P(("grp", "blk")), check_vma=False
    )
```

time: 40.5 us -> 46 us (1.14)
  Pallas kernels: 37.9 us -> 44.6 us
  local copies, waits for them, and re-layouts: 2.41 us -> 1.22 us
    pallas_call x1, Pallas kernels: 37.9 us -> 44.6 us  [local(): pl.pallas_call(functools.partial(kernel, groups, blocks), out_shape=jax.S...]
    unnamed x9 -> x3, local copies, waits for them, and re-layouts: 2.41 us -> 1.22 us
where the time goes in v2:
time: 46 us; the launch traced here: 45.9 us
  Pallas kernels  44.6 us (97%)
  local copies, waits for them, and re-layouts  1.22 us (3%)
    pallas_call x1, Pallas kernels, local(): pl.pallas_call(functools.partial(kernel, groups, blocks), out_shape=jax.S...  44.6 us
    unnamed x3, local copies, waits for them, and re-layouts  1.22 us

profile of v2, /device:TPU:0, one launch (start us, length us, event | category | flops | bytes accessed | tf_op | source)
XLA Modules:
  0.0 45.9 jit_solution(12892148657731721836)
XLA Ops:
  0.0 44.6 %shard_map.46 = f32[1,256]{1,0:T(1,128)} custom-call(f32[256,768]{1,0:T(8,128)} %emb_h.1, s32[1,256]{1,0:T(1,128)} %bitcast.5, s32[1,256]{1,0:T(1,128)} %bitcast.6, s32[1,256]{1,0:T(1,128)} %bitcast.7), custom_call_target="tpu_custom_call" | custom-call | tf_op jit(solution)/shard_map/pallas_call | solution.py:331
  44.6 0.0 copy-start
  44.7 0.7 %copy-done = f32[1,256]{1,0:T(1,128)S(1)} copy-done((f32[1,256]{1,0:T(1,128)S(1)}, f32[1,256]{1,0:T(1,128)}, u32[]{:S(2)}) %copy-start) | copy-done | bytes 1048
  45.3 0.6 %copy.6 = f32[256]{0:T(256)} copy(f32[256]{0:T(256)S(1)} %bitcast.4) | data formatting | bytes 2048
Async XLA Ops:
  44.6 0.7 %copy-start = (f32[1,256]{1,0:T(1,128)S(1)}, f32[1,256]{1,0:T(1,128)}, u32[]{:S(2)}) copy-start(f32[1,256]{1,0:T(1,128)} %shard_map.46) | copy-start | bytes 3076

commit v3 on v2

--- a/solution.py
+++ b/solution.py
@@ -113,6 +113,12 @@
 
     above, below = device(x, y, c, lax.rem(z + 1, zs)), device(x, y, c, lax.rem(z + zs - 1, zs))
 
+    for d in range(1, ps):
+        p = lax.rem(me + d, ps)
+        copy(meta_p.at[me], meta_p.at[me], meta_recv_p.at[me], plane_device(p))
+    for d in range(1, zs):
+        to = device(x, y, c, lax.rem(z + d, zs))
+        copy(meta_z.at[z], meta_z.at[z], meta_recv_z.at[z], to)
     for q in range(CHUNKS):
         copy(own(q), slot(0, q), up_recv.at[0, q], above, z < mid)
         if downs:
@@ -121,12 +127,6 @@
         send_piece(me, hx, to_x)
         for d in range(1, ys):
             send_piece(me, hy, device(x, y_peer(d), c, z))
-    for d in range(1, ps):
-        p = lax.rem(me + d, ps)
-        copy(meta_p.at[me], meta_p.at[me], meta_recv_p.at[me], plane_device(p))
-    for d in range(1, zs):
-        to = device(x, y, c, lax.rem(z + d, zs))
-        copy(meta_z.at[z], meta_z.at[z], meta_recv_z.at[z], to)
     for h in (0, 1):
         send_piece(me, h, to_c)
 
@@ -239,16 +239,18 @@
 
     row_acc[...] = jnp.full(row_acc.shape, -1.0, jnp.float32)
     col_wide[...] = jnp.full(col_wide.shape, -1.0, jnp.float32)
-    for d in range(1, zs):
-        o = lax.rem(z + d, zs)
-        arrived(meta_z.at[o], meta_recv_z.at[o])
-    for o in range(zs):
-        m = meta_z[o]
-        col_lo[o] = jnp.broadcast_to(m[0:1], (128, n)).T
-        col_key[o] = jnp.broadcast_to(m[1:2], (128, n)).T
-    for d in range(1, ps):
-        p = lax.rem(me + d, ps)
-        arrived(meta_p.at[p], meta_recv_p.at[p])
+
+    def keys():
+        for d in range(1, ps):
+            p = lax.rem(me + d, ps)
+            arrived(meta_p.at[p], meta_recv_p.at[p])
+        for d in range(1, zs):
+            o = lax.rem(z + d, zs)
+            arrived(meta_z.at[o], meta_recv_z.at[o])
+        for o in range(zs):
+            m = meta_z[o]
+            col_lo[o] = jnp.broadcast_to(m[0:1], (128, n)).T
+            col_key[o] = jnp.broadcast_to(m[1:2], (128, n)).T
 
     last = ups - 1
     for t in range(ups):
@@ -256,6 +258,7 @@
             step_line(t, q)
             if (t, q) == (0, 1):
                 early_plane()
+                keys()
             if (t, q) == (0, CHUNKS - 1):
                 late_plane()
                 compute_own(near)

time: 46 us -> 39.2 us (0.85)
  Pallas kernels: 44.6 us -> 37.8 us
    pallas_call x1, Pallas kernels: 44.6 us -> 37.8 us  [local(): pl.pallas_call(functools.partial(kernel, groups, blocks), out_shape=jax.S...]
where the time goes in v3:
time: 39.2 us; the launch traced here: 39 us
  Pallas kernels  37.8 us (96%)
  local copies, waits for them, and re-layouts  1.22 us (3%)
    pallas_call x1, Pallas kernels, local(): pl.pallas_call(functools.partial(kernel, groups, blocks), out_shape=jax.S...  37.8 us
    unnamed x3, local copies, waits for them, and re-layouts  1.22 us

profile of v3, /device:TPU:0, one launch (start us, length us, event | category | flops | bytes accessed | tf_op | source)
XLA Modules:
  0.0 39.0 jit_solution(1145398837716927928)
XLA Ops:
  0.0 37.8 %shard_map.46 = f32[1,256]{1,0:T(1,128)} custom-call(f32[256,768]{1,0:T(8,128)} %emb_h.1, s32[1,256]{1,0:T(1,128)} %bitcast.5, s32[1,256]{1,0:T(1,128)} %bitcast.6, s32[1,256]{1,0:T(1,128)} %bitcast.7), custom_call_target="tpu_custom_call" | custom-call | tf_op jit(solution)/shard_map/pallas_call | solution.py:334
  37.8 0.0 copy-start
  37.8 0.7 %copy-done = f32[1,256]{1,0:T(1,128)S(1)} copy-done((f32[1,256]{1,0:T(1,128)S(1)}, f32[1,256]{1,0:T(1,128)}, u32[]{:S(2)}) %copy-start) | copy-done | bytes 1048
  38.5 0.6 %copy.6 = f32[256]{0:T(256)} copy(f32[256]{0:T(256)S(1)} %bitcast.4) | data formatting | bytes 2048
Async XLA Ops:
  37.8 0.7 %copy-start = (f32[1,256]{1,0:T(1,128)S(1)}, f32[1,256]{1,0:T(1,128)}, u32[]{:S(2)}) copy-start(f32[1,256]{1,0:T(1,128)} %shard_map.46) | copy-start | bytes 3076

commit v4 on v3

--- a/solution.py
+++ b/solution.py
@@ -122,7 +122,7 @@
     for q in range(CHUNKS):
         copy(own(q), slot(0, q), up_recv.at[0, q], above, z < mid)
         if downs:
-            copy(own(q), slot(ups, q), down_recv.at[0, q], below, z > mid)
+            copy(own(q), slot(ups, q), down_recv.at[0, q], below, z >= mid)
     for hx, hy in ((0, 1), (1, 0)):
         send_piece(me, hx, to_x)
         for d in range(1, ys):
@@ -134,7 +134,7 @@
         return z > t
 
     def has_down(t):
-        return (z >= mid) & (zs - 1 - z > t)
+        return (z < mid) | (zs - 1 - z > t)
 
     def step_line(t, q):
         if t < ups:
@@ -151,7 +151,8 @@
                 arrived(slot(ups + t, q), down_recv.at[t, q])
             if t + 1 < downs:
                 copy(slot(ups + t, q), slot(ups + t + 1, q), down_recv.at[t + 1, q], below,
-                     has_down(t) & (z > mid))
+                     has_down(t) & (z >= mid))
+            copy(slot(ups + t, q), slot(ups + t, q), down_recv.at[t, q], below, (z > 0) & (z < mid))
 
     def nth(j):
         k = j // 2
@@ -192,7 +193,7 @@
         compute(rows.at[me], z, 0, n, members, False)
 
     def compute_up(t, members, start=0, count=n):
-        @pl.when(has_up(t))
+        @pl.when(has_up(t) & ((z < mid) | (z == zs - 1)))
         def _():
             compute(line.at[t], jnp.minimum(z, mid) - 1 - t, start, count, members, True)
 
@@ -200,7 +201,7 @@
         if t < downs:
             @pl.when(has_down(t))
             def _():
-                compute(line.at[ups + t], z + 1 + t, 0, n, members, True)
+                compute(line.at[ups + t], jnp.maximum(z + 1, mid) + t, 0, n, members, True)
 
     def early_plane():
         wait_piece(place(x_other, y, c), 0)
@@ -295,9 +296,9 @@
             recv_sem=row_recv.at[me], device_id=plane_device(p), device_id_type=MESH)
 
     for o in range(zs):
-        finish_line(o, z != o if o else (z > 0) & (z < mid))
+        finish_line(o, z != o if o else (z > 0) & (z < zs - 1))
     compute_up(last, every, half, half)
-    finish_line(0, z >= mid)
+    finish_line(0, z == zs - 1)
     for d in range(1, ps):
         plane_home(lax.rem(me + d, ps)).start()
     best = jnp.maximum(row_acc[me], fold(col_wide[z].T))
@@ -329,7 +330,7 @@
     slots = mid + max(1, zs - mid - 1)
     f32, bf16 = jnp.float32, jnp.bfloat16
     sends = (ps + zs + CHUNKS * 2 + 4 + 2 * ys + 2 + ys + 3 * ys + 2 * ys
-             + 3 * CHUNKS * slots)
+             + 4 * CHUNKS * slots)
     dma = pltpu.SemaphoreType.DMA
     found = pl.pallas_call(
         functools.partial(kernel, groups, blocks),

time: 39.2 us -> 39.1 us (level)
  no operation moved by 1% of the time
where the time goes in v4:
time: 39.1 us; the launch traced here: 39 us
  Pallas kernels  37.7 us (96%)
  local copies, waits for them, and re-layouts  1.22 us (3%)
    pallas_call x1, Pallas kernels, local(): pl.pallas_call(functools.partial(kernel, groups, blocks), out_shape=jax.S...  37.7 us
    unnamed x3, local copies, waits for them, and re-layouts  1.22 us

profile of v4, /device:TPU:0, one launch (start us, length us, event | category | flops | bytes accessed | tf_op | source)
XLA Modules:
  0.0 39.0 jit_solution(6328223086703305157)
XLA Ops:
  0.0 37.7 %shard_map.46 = f32[1,256]{1,0:T(1,128)} custom-call(f32[256,768]{1,0:T(8,128)} %emb_h.1, s32[1,256]{1,0:T(1,128)} %bitcast.5, s32[1,256]{1,0:T(1,128)} %bitcast.6, s32[1,256]{1,0:T(1,128)} %bitcast.7), custom_call_target="tpu_custom_call" | custom-call | tf_op jit(solution)/shard_map/pallas_call | solution.py:335
  37.8 0.0 copy-start
  37.8 0.7 %copy-done = f32[1,256]{1,0:T(1,128)S(1)} copy-done((f32[1,256]{1,0:T(1,128)S(1)}, f32[1,256]{1,0:T(1,128)}, u32[]{:S(2)}) %copy-start) | copy-done | bytes 1048
  38.4 0.6 %copy.6 = f32[256]{0:T(256)} copy(f32[256]{0:T(256)S(1)} %bitcast.4) | data formatting | bytes 2048
Async XLA Ops:
  37.8 0.7 %copy-start = (f32[1,256]{1,0:T(1,128)S(1)}, f32[1,256]{1,0:T(1,128)}, u32[]{:S(2)}) copy-start(f32[1,256]{1,0:T(1,128)} %shard_map.46) | copy-start | bytes 3076

commit v5 on v4

--- a/solution.py
+++ b/solution.py
@@ -123,10 +123,10 @@
         copy(own(q), slot(0, q), up_recv.at[0, q], above, z < mid)
         if downs:
             copy(own(q), slot(ups, q), down_recv.at[0, q], below, z >= mid)
-    for hx, hy in ((0, 1), (1, 0)):
-        send_piece(me, hx, to_x)
-        for d in range(1, ys):
-            send_piece(me, hy, device(x, y_peer(d), c, z))
+        if q % 2 == 0:
+            send_piece(me, q // 2, to_x)
+            for d in range(1, ys):
+                send_piece(me, 1 - q // 2, device(x, y_peer(d), c, z))
     for h in (0, 1):
         send_piece(me, h, to_c)
 
@@ -266,17 +266,22 @@
             if (t, q) == (1, 0):
                 compute_up(0, near)
             if (t, q) == (1, 1):
-                far_plane()
                 compute_down(0, near)
             if (t, q) == (1, 2):
+                far_plane()
+                if last == 1:
+                    compute_up(last, near, 0, half)
+            if t > 1 and q == 1:
+                compute_up(t - 1, every)
+                compute_down(t - 1, every)
+            if (t, q) == (1, CHUNKS - 1):
                 far_sibling()
                 compute_own(far)
                 compute_up(0, far)
                 compute_down(0, far)
-            if t > 1 and q == 1:
-                compute_up(t - 1, every)
-                compute_down(t - 1, every)
-            if (t, q) == (last, 2):
+                if last == 1:
+                    compute_up(last, far, 0, half)
+            if last > 1 and (t, q) == (last, 2):
                 compute_up(last, every, 0, half)
 
     def line_home(o):

time: 39.1 us -> 40.1 us (1.026)
  Pallas kernels: 37.7 us -> 38.7 us
    pallas_call x1, Pallas kernels: 37.7 us -> 38.7 us  [local(): pl.pallas_call(functools.partial(kernel, groups, blocks), out_shape=jax.S...]
where the time goes in v5:
time: 40.1 us; the launch traced here: 39.9 us
  Pallas kernels  38.7 us (97%)
  local copies, waits for them, and re-layouts  1.22 us (3%)
    pallas_call x1, Pallas kernels, local(): pl.pallas_call(functools.partial(kernel, groups, blocks), out_shape=jax.S...  38.7 us
    unnamed x3, local copies, waits for them, and re-layouts  1.22 us

profile of v5, /device:TPU:0, one launch (start us, length us, event | category | flops | bytes accessed | tf_op | source)
XLA Modules:
  0.0 39.9 jit_solution(9846012025935945057)
XLA Ops:
  0.0 38.7 %shard_map.46 = f32[1,256]{1,0:T(1,128)} custom-call(f32[256,768]{1,0:T(8,128)} %emb_h.1, s32[1,256]{1,0:T(1,128)} %bitcast.5, s32[1,256]{1,0:T(1,128)} %bitcast.6, s32[1,256]{1,0:T(1,128)} %bitcast.7), custom_call_target="tpu_custom_call" | custom-call | tf_op jit(solution)/shard_map/pallas_call | solution.py:340
  38.7 0.0 copy-start
  38.7 0.7 %copy-done = f32[1,256]{1,0:T(1,128)S(1)} copy-done((f32[1,256]{1,0:T(1,128)S(1)}, f32[1,256]{1,0:T(1,128)}, u32[]{:S(2)}) %copy-start) | copy-done | bytes 1048
  39.3 0.6 %copy.6 = f32[256]{0:T(256)} copy(f32[256]{0:T(256)S(1)} %bitcast.4) | data formatting | bytes 2048
Async XLA Ops:
  38.7 0.7 %copy-start = (f32[1,256]{1,0:T(1,128)S(1)}, f32[1,256]{1,0:T(1,128)}, u32[]{:S(2)}) copy-start(f32[1,256]{1,0:T(1,128)} %shard_map.46) | copy-start | bytes 3076

commit v6 on v4

--- a/solution.py
+++ b/solution.py
@@ -123,12 +123,12 @@
         copy(own(q), slot(0, q), up_recv.at[0, q], above, z < mid)
         if downs:
             copy(own(q), slot(ups, q), down_recv.at[0, q], below, z >= mid)
-    for hx, hy in ((0, 1), (1, 0)):
+    def send_own(hx, hy):
         send_piece(me, hx, to_x)
         for d in range(1, ys):
             send_piece(me, hy, device(x, y_peer(d), c, z))
-    for h in (0, 1):
-        send_piece(me, h, to_c)
+
+    send_own(0, 1)
 
     def has_up(t):
         return z > t
@@ -258,7 +258,10 @@
         for q in range(CHUNKS):
             step_line(t, q)
             if (t, q) == (0, 1):
+                send_own(1, 0)
                 early_plane()
+                for h in (0, 1):
+                    send_piece(me, h, to_c)
                 keys()
             if (t, q) == (0, CHUNKS - 1):
                 late_plane()
@@ -310,7 +313,7 @@
         p = lax.rem(me + d, ps)
         arrived(row_in.at[p], row_recv.at[p])
         best = jnp.maximum(best, row_in[p])
-    out[...] = jnp.max(best, axis=0, keepdims=True)
+    out[...] = best
 
     for made, cond in started:
         if cond is None:
@@ -334,7 +337,7 @@
     dma = pltpu.SemaphoreType.DMA
     found = pl.pallas_call(
         functools.partial(kernel, groups, blocks),
-        out_shape=jax.ShapeDtypeStruct((1, n), f32),
+        out_shape=jax.ShapeDtypeStruct((8, n), f32),
         in_specs=[pl.BlockSpec(memory_space=pltpu.HBM)] * 4,
         out_specs=pl.BlockSpec(memory_space=pltpu.VMEM),
         scratch_shapes=[
@@ -366,7 +369,7 @@
         compiler_params=pltpu.CompilerParams(
             collective_id=0, has_side_effects=True, vmem_limit_bytes=64 * 1024 * 1024 - 524288),
     )(embeddings, owner.reshape(1, n), cluster.reshape(1, n), order.reshape(1, n))
-    return found.reshape(n)
+    return jnp.max(found, axis=0)
 
 
 def solution(mesh):

time: 39.1 us -> 41.6 us (1.064)
  Pallas kernels: 37.7 us -> 40.1 us
  other arithmetic: 0 us -> 1.27 us
  local copies, waits for them, and re-layouts: 1.22 us -> 0 us
    pallas_call x1, Pallas kernels: 37.7 us -> 40.1 us  [local(): pl.pallas_call(functools.partial(kernel, groups, blocks), out_shape=jax.S...]
    reduce_max x0 -> x1, other arithmetic: none -> 1.27 us  [local(): return jnp.max(found, axis=0)]
    unnamed x3 -> x0, local copies, waits for them, and re-layouts: 1.22 us -> none
where the time goes in v6:
time: 41.6 us; the launch traced here: 41.4 us
  Pallas kernels  40.1 us (96%)
  other arithmetic  1.27 us (3%)
    pallas_call x1, Pallas kernels, local(): pl.pallas_call(functools.partial(kernel, groups, blocks), out_shape=jax.S...  40.1 us
    reduce_max x1, other arithmetic, local(): return jnp.max(found, axis=0)  1.27 us

profile of v6, /device:TPU:0, one launch (start us, length us, event | category | flops | bytes accessed | tf_op | source)
XLA Modules:
  0.0 41.4 jit_solution(5924922047921449369)
XLA Ops:
  0.0 40.1 %shard_map.46 = f32[8,256]{1,0:T(8,128)} custom-call(f32[256,768]{1,0:T(8,128)} %emb_h.1, s32[1,256]{1,0:T(1,128)} %bitcast.3, s32[1,256]{1,0:T(1,128)} %bitcast.4, s32[1,256]{1,0:T(1,128)} %bitcast.5), custom_call_target="tpu_custom_call" | custom-call | tf_op jit(solution)/shard_map/pallas_call | solution.py:338
  40.1 1.3 %reduce_max.9 = f32[256]{0:T(256)} reduce(f32[8,256]{1,0:T(8,128)} %shard_map.46, f32[]{:T(128)} %constant.0.clone.1), dimensions={0}, to_apply=%region_0.0 | reduce | flops 1792 | bytes 9220 | tf_op jit(solution)/shard_map/reduce_max | solution.py:372

commit v7 on v4

--- a/solution.py
+++ b/solution.py
@@ -266,9 +266,13 @@
             if (t, q) == (1, 0):
                 compute_up(0, near)
             if (t, q) == (1, 1):
+                compute_down(0, near)
+            if (t, q) == (1, 2) and last == 1:
+                compute_up(last, near, 0, half)
+            if (t, q) == (1, CHUNKS - 1):
                 far_plane()
-                compute_down(0, near)
-            if (t, q) == (1, 2):
+                if last == 1:
+                    compute_up(last, near, half, half)
                 far_sibling()
                 compute_own(far)
                 compute_up(0, far)
@@ -276,7 +280,7 @@
             if t > 1 and q == 1:
                 compute_up(t - 1, every)
                 compute_down(t - 1, every)
-            if (t, q) == (last, 2):
+            if (t, q) == (last, 2) and last > 1:
                 compute_up(last, every, 0, half)
 
     def line_home(o):
@@ -297,7 +301,10 @@
 
     for o in range(zs):
         finish_line(o, z != o if o else (z > 0) & (z < zs - 1))
-    compute_up(last, every, half, half)
+    if last > 1:
+        compute_up(last, every, half, half)
+    else:
+        compute_up(last, far)
     finish_line(0, z == zs - 1)
     for d in range(1, ps):
         plane_home(lax.rem(me + d, ps)).start()

time: 39.1 us -> 40 us (1.023)
  Pallas kernels: 37.7 us -> 38.6 us
    pallas_call x1, Pallas kernels: 37.7 us -> 38.6 us  [local(): pl.pallas_call(functools.partial(kernel, groups, blocks), out_shape=jax.S...]
where the time goes in v7:
time: 40 us; the launch traced here: 39.9 us
  Pallas kernels  38.6 us (96%)
  local copies, waits for them, and re-layouts  1.22 us (3%)
    pallas_call x1, Pallas kernels, local(): pl.pallas_call(functools.partial(kernel, groups, blocks), out_shape=jax.S...  38.6 us
    unnamed x3, local copies, waits for them, and re-layouts  1.22 us

profile of v7, /device:TPU:0, one launch (start us, length us, event | category | flops | bytes accessed | tf_op | source)
XLA Modules:
  0.0 39.9 jit_solution(12033760482718776461)
XLA Ops:
  0.0 38.6 %shard_map.46 = f32[1,256]{1,0:T(1,128)} custom-call(f32[256,768]{1,0:T(8,128)} %emb_h.1, s32[1,256]{1,0:T(1,128)} %bitcast.5, s32[1,256]{1,0:T(1,128)} %bitcast.6, s32[1,256]{1,0:T(1,128)} %bitcast.7), custom_call_target="tpu_custom_call" | custom-call | tf_op jit(solution)/shard_map/pallas_call | solution.py:342
  38.7 0.0 copy-start
  38.7 0.7 %copy-done = f32[1,256]{1,0:T(1,128)S(1)} copy-done((f32[1,256]{1,0:T(1,128)S(1)}, f32[1,256]{1,0:T(1,128)}, u32[]{:S(2)}) %copy-start) | copy-done | bytes 1048
  39.3 0.6 %copy.6 = f32[256]{0:T(256)} copy(f32[256]{0:T(256)S(1)} %bitcast.4) | data formatting | bytes 2048
Async XLA Ops:
  38.7 0.7 %copy-start = (f32[1,256]{1,0:T(1,128)S(1)}, f32[1,256]{1,0:T(1,128)}, u32[]{:S(2)}) copy-start(f32[1,256]{1,0:T(1,128)} %shard_map.46) | copy-start | bytes 3076
